TPU v7x, 32 devices: a whole 2x2x4 slice. The times are simulated.
32 devices in a mesh: groups: 2 (over x), fsdp: 4 (over y, core), tp: 4 (over z).
Axes of the slice: x: 2, y: 2, z: 4, core: 2. Of those that a mesh axis runs over, the one named last changes fastest.
Arguments:
- layer_inputs: bfloat16 [4, 768, 4608], P(None, ('groups', 'fsdp'), 'tp'), parts along dimension 1, may hold values from -6 to 6
- norm_gain: bfloat16 [4608], replicated, may hold values from 0.099609375 to 1.8984375
- query_weight: bfloat16 [4608, 2048], P(None, 'tp'), may hold values from -0.75 to 0.75
- key_weight: bfloat16 [4608, 1024], P(None, 'tp'), may hold values from -0.09375 to 0.09375
- value_weight: bfloat16 [4608, 1024], P(None, 'tp'), may hold values from -0.09375 to 0.09375
- output_weight: bfloat16 [2048, 4608], P('tp'), may hold values from -0.5 to 0.5
- query_down: bfloat16 [9216, 64], P(('groups', 'fsdp')), parts along dimension 0, may hold values from -0.75 to 0.75
- key_down: bfloat16 [9216, 64], P(('groups', 'fsdp')), parts along dimension 0, may hold values from -0.09375 to 0.09375
- value_down: bfloat16 [9216, 64], P(('groups', 'fsdp')), parts along dimension 0, may hold values from -0.09375 to 0.09375
- output_down: bfloat16 [4096, 64], P(('groups', 'fsdp')), parts along dimension 0, may hold values from -0.125 to 0.125
- query_up: bfloat16 [4096, 64], P(('groups', 'fsdp')), parts along dimension 0, may hold values from -0.375 to 0.375
- key_up_factor: bfloat16 [2048, 64], P(('groups', 'fsdp')), parts along dimension 0, may hold values from -0.375 to 0.375
- value_up: bfloat16 [2048, 64], P(('groups', 'fsdp')), parts along dimension 0, may hold values from -0.375 to 0.375
- output_up: bfloat16 [9216, 64], P(('groups', 'fsdp')), parts along dimension 0, may hold values from -0.375 to 0.375
- cached_keys: bfloat16 [768, 8, 96, 128], P(('groups', 'fsdp'), 'tp'), parts along dimension 0, may hold values from -9 to 9
- cached_values: bfloat16 [768, 8, 96, 128], P(('groups', 'fsdp'), 'tp'), parts along dimension 0, may hold values from -6 to 6
- context_lengths: int32 [768], P(('groups', 'fsdp')), parts along dimension 0, may hold values from 1 to 96, as said below
Outputs:
- attention_out: bfloat16 [4, 768, 4608], P(None, ('groups', 'fsdp'), 'tp'), parts along dimension 1
There are 2 independent parts, one for each index of `groups`. A program takes and returns all parts, laid end to end along the dimension named above; an argument that names none is the same for every part. Nothing has to cross between parts.
Inputs may be any that keep to these rules, and one draw needn't show every extreme that they name: `context_lengths`: in each aligned block of 96 rows, at least one row has all 96 slots live.
All inputs are finite; a program needn't handle non-finite values.
Results may differ from a plain program's by a relative error of at most 0.012.
The roundings to bfloat16 on the way count: a program that leaves them out, or rounds other values in their place, can miss the bound.
Values may be sent and summed in bfloat16 or wider, within the bound.
A program may use at most 128 MiB of HBM per device.

v0:
```python
import functools

import jax
import jax.numpy as jnp
from jax import lax
from jax.experimental import pallas as pl
from jax.experimental.pallas import tpu as pltpu
from jax.sharding import PartitionSpec as P

HEADS = 16
KV_HEADS = 8
HF = 128
STEPS = 4
CHUNK = 32

ADAPTER_SCALE = 2.0
SOFTCAP = 50.0
QUERY_SCALE = 144.0 ** (-0.5)
RMS_EPS = 1e-06
ROPE_BASE = 10000.0


def merged(base_weight, down, up):
    weight_update = jnp.dot(down, up.T, preferred_element_type=jnp.float32)
    return (base_weight.astype(jnp.float32) + ADAPTER_SCALE * weight_update).astype(jnp.bfloat16)


def rope_tables(context_lengths):
    half = HF // 2
    freq = ROPE_BASE ** (-2.0 * jnp.arange(half, dtype=jnp.float32) / HF)
    steps = jnp.arange(STEPS, dtype=jnp.int32)
    position = (context_lengths[None, :] + steps[:, None]).astype(jnp.float32)
    angle = position[..., None] * freq
    cosine = jnp.cos(angle)
    sine = jnp.sin(angle)
    return (
        jnp.concatenate([cosine, cosine], axis=-1),
        jnp.concatenate([-sine, sine], axis=-1),
    )


def attend_chunk(kv_local, load, cos, sin, lens, ck_ref, cv_ref, store, q3, k3, v3, a3):
    per = HEADS // KV_HEADS
    for s in range(STEPS):
        c, n = cos(s), sin(s)

        def rot(u):
            return u * c + pltpu.roll(u, HF // 2, 1) * n

        for g in range(kv_local):
            for p in range(per):
                u = rot(load(0, s, g * per + p)) * QUERY_SCALE
                q3[:, g * 8 + s * per + p, :] = u
            k3[:, g * 8 + s, :] = rot(load(1, s, g))
            v3[:, g * 8 + s, :] = load(2, s, g)

    slot = lax.broadcasted_iota(jnp.int32, (8, HF), 1)
    step_of = lax.broadcasted_iota(jnp.int32, (8, HF), 0) // per
    ctx = ck_ref.shape[2]
    new_live = (slot >= ctx) & (slot <= ctx + step_of)
    pad = jnp.zeros((HF - ctx - 8, HF), jnp.float32)
    group = 4

    def body(i, carry):
        for j in range(group):
            r = i * group + j
            live = new_live | (slot < lens(r))
            for g in range(kv_local):
                q = q3[r, pl.ds(g * 8, 8), :].astype(jnp.bfloat16)
                kn = jnp.concatenate([k3[r, pl.ds(g * 8, 8), :], pad]).astype(jnp.bfloat16)
                vn = jnp.concatenate([v3[r, pl.ds(g * 8, 8), :], pad]).astype(jnp.bfloat16)
                keys = jnp.concatenate([ck_ref[r, g], kn])
                values = jnp.concatenate([cv_ref[r, g], vn])
                score = lax.dot_general(
                    q, keys, (((1,), (1,)), ((), ())), preferred_element_type=jnp.float32
                )
                expo = jnp.where(live, jnp.exp(SOFTCAP * jnp.tanh(score / SOFTCAP)), 0.0)
                total = jnp.sum(expo, axis=-1, keepdims=True)
                weight = (expo / total).astype(jnp.bfloat16)
                a3[r, pl.ds(g * 8, 8), :] = jnp.dot(
                    weight, values, preferred_element_type=jnp.float32
                )
        return carry

    lax.fori_loop(0, CHUNK // group, body, 0)
    for s in range(STEPS):
        for g in range(kv_local):
            for p in range(per):
                store(s, g * per + p, a3[:, g * 8 + s * per + p, :].astype(jnp.bfloat16))


def attention_kernel(kv_local, lens_ref, q_ref, k_ref, v_ref, cos_ref, sin_ref, ck_ref, cv_ref, o_ref, q3, k3, v3, a3):
    k3[...] = jnp.zeros_like(k3)
    v3[...] = jnp.zeros_like(v3)
    base = pl.program_id(0) * CHUNK
    refs = (q_ref, k_ref, v_ref)

    def load(which, s, h):
        return refs[which][s, :, pl.ds(h * HF, HF)]

    def store(s, h, value):
        o_ref[s, :, pl.ds(h * HF, HF)] = value

    attend_chunk(
        kv_local, load, lambda s: cos_ref[s], lambda s: sin_ref[s],
        lambda r: lens_ref[base + r], ck_ref, cv_ref, store, q3, k3, v3, a3,
    )


def attention(lens, q, k, v, cos, sin, ck, cv):
    rows = lens.shape[0]
    kv_local = ck.shape[1]
    ql, kl = q.shape[-1], k.shape[-1]
    tok = lambda w: pl.BlockSpec((STEPS, CHUNK, w), lambda i, *_: (0, i, 0))
    cache = pl.BlockSpec((CHUNK,) + ck.shape[1:], lambda i, *_: (i, 0, 0, 0))
    scratch = pltpu.VMEM((CHUNK, kv_local * 8, HF), jnp.float32)
    return pl.pallas_call(
        functools.partial(attention_kernel, kv_local),
        out_shape=jax.ShapeDtypeStruct((STEPS, rows, ql), jnp.bfloat16),
        grid_spec=pltpu.PrefetchScalarGridSpec(
            num_scalar_prefetch=1,
            grid=(rows // CHUNK,),
            in_specs=[tok(ql), tok(kl), tok(kl), tok(HF), tok(HF), cache, cache],
            out_specs=tok(ql),
            scratch_shapes=[scratch] * 4,
        ),
        compiler_params=pltpu.CompilerParams(vmem_limit_bytes=40 * 2**20),
    )(lens, q, k, v, cos, sin, ck, cv)


def shards(
    x, norm_gain, query_weight, key_weight, value_weight, output_weight,
    query_down, key_down, value_down, output_down,
    query_up, key_up_factor, value_up, output_up,
    cached_keys, cached_values, context_lengths,
):
    tp_rank = lax.axis_index("tp")
    n_fsdp = lax.axis_size("fsdp")
    nrows = x.shape[1]
    ql, kl = query_weight.shape[1], key_weight.shape[1]
    sizes = [query_down.shape[0], value_down.shape[0], output_down.shape[0], key_up_factor.shape[0]]
    pack = jnp.concatenate([
        jnp.concatenate([query_down, key_down], 1),
        jnp.concatenate([value_down, output_up], 1),
        jnp.concatenate([output_down, query_up], 1),
        jnp.concatenate([key_up_factor, value_up], 1),
    ])
    every = lax.all_gather(pack, "fsdp", axis=0)
    xs = lax.all_gather(x, "tp", axis=2, tiled=True)
    rank = query_down.shape[1]
    ends = [0]
    for size in sizes:
        ends.append(ends[-1] + size)
    parts = [every[:, a:b].reshape(-1, 2 * rank) for a, b in zip(ends[:-1], ends[1:])]

    def block(whole, width):
        return lax.dynamic_slice_in_dim(whole, tp_rank * width, width, 0)

    third = block(parts[2], ql)
    fourth = block(parts[3], kl)
    w_query = merged(query_weight, parts[0][:, :rank], third[:, rank:])
    w_key = merged(key_weight, parts[0][:, rank:], fourth[:, :rank])
    w_value = merged(value_weight, parts[1][:, :rank], fourth[:, rank:])
    w_output = merged(output_weight, third[:, :rank], parts[1][:, rank:])
    wide = xs.astype(jnp.float32)
    factor = lax.rsqrt(jnp.mean(wide * wide, axis=-1, keepdims=True) + RMS_EPS)
    normed = (wide * factor * norm_gain.astype(jnp.float32)).astype(jnp.bfloat16)
    q = jnp.dot(normed, w_query, preferred_element_type=jnp.float32)
    k = jnp.dot(normed, w_key, preferred_element_type=jnp.float32)
    v = jnp.dot(normed, w_value, preferred_element_type=jnp.float32)
    cos, sin = rope_tables(context_lengths)
    attended = attention(context_lengths, q, k, v, cos, sin, cached_keys, cached_values)
    terms = jnp.dot(attended, w_output, preferred_element_type=jnp.float32)
    return lax.psum_scatter(terms.astype(jnp.bfloat16), "tp", scatter_dimension=2, tiled=True)


def solution(mesh):
    fs = ("groups", "fsdp")
    return jax.shard_map(
        shards,
        mesh=mesh,
        in_specs=(
            P(None, fs, "tp"), P(),
            P(None, "tp"), P(None, "tp"), P(None, "tp"), P("tp", None),
            P(fs, None), P(fs, None), P(fs, None), P(fs, None),
            P(fs, None), P(fs, None), P(fs, None), P(fs, None),
            P(fs, "tp", None, None), P(fs, "tp", None, None), P(fs),
        ),
        out_specs=P(None, fs, "tp"),
        check_vma=False,
    )
```

profile of v0, /device:TPU:0, one launch (start us, length us, event | category | flops | bytes accessed | tf_op | source)
XLA Modules:
  0.0 288.0 jit_solution(17678104238042033419)
XLA Ops:
  6.5 0.0 all-gather.6.cloned.1.call-start
  6.5 2.2 maximum_maximum_fusion
  8.7 0.0 all-gather.6.cloned.1.call-update
  8.8 0.0 all-gather.4.cloned.1.call-start
  8.8 0.7 all-gather.4.cloned.1.call-update
  9.5 0.0 reduce-scatter.4.cloned.1.call-start
  9.6 1.3 convert_element_type.44
  10.9 0.7 add_convert_fusion.2
  11.5 0.8 fusion.29
  12.3 0.2 pad_maximum_fusion
  12.5 27.7 %all-gather.6.cloned.1.call-done = bf16[12288,128]{0,1:T(8,128)(2,1)} async-done(((bf16[3072,128]{0,1:T(8,128)(2,1)}), bf16[12288,128]{0,1:T(8,128)(2,1)}) %all-gather.6.cloned.1.call-update) | async-done | bytes 3145744 | tf_op jit(solution)/shard_map/all_gather | solution.py:148
  40.2 6.3 %reshape.49 = bf16[4,3072,128]{1,0,2:T(4,128)(2,1)S(1)} reshape(bf16[12288,128]{0,1:T(8,128)(2,1)} %all-gather.6.cloned.1.call-done) | data formatting | bytes 6291456 | tf_op jit(solution)/shard_map/all_gather | solution.py:148
  46.5 0.1 slice.52
  46.6 0.2 slice.50
  46.7 0.7 copy.22
  47.5 0.8 fusion.42
  48.3 0.1 copy.23
  48.4 0.0 copy-start.4
  48.4 0.1 copy.20
  48.6 0.0 copy-start.3
  48.6 1.0 copy.21
  49.6 62.2 %all-gather.4.cloned.1.call-done = bf16[4,96,4608]{2,1,0:T(8,128)(2,1)} async-done(((bf16[4,96,1152]{2,1,0:T(8,128)(2,1)}), bf16[4,96,4608]{2,1,0:T(8,128)(2,1)}) %all-gather.4.cloned.1.call-update) | async-done | bytes 3538960 | tf_op jit(solution)/shard_map/all_gather | solution.py:149
  111.7 2.8 fusion
  114.5 0.0 copy-done.4
  114.5 4.9 %fusion.13.k_ref = f32[4,96,256]{2,1,0:T(8,128)S(1)} fusion(bf16[4,96,4608]{2,1,0:T(8,128)(2,1)} %all-gather.4.cloned.1.call-done, f32[4608]{0:T(1024)S(1)} %copy-done.4, f32[4,96]{1,0:T(4,128)S(1)} %add_rsqrt_fusion, bf16[4608,256]{1,0:T(8,128)(2,1)} %param.20, bf16[4608,128]{0,1:T(8,128)(2,1)S(1)} %bitcast.44, bf16[1024,128]{0,1:T(8,128)(2,1)} %bitcast.49, ...), kind=kOutput, calls=%fused_computation.19 | convolution fusion | flops 1068761088 | bytes 6936580 | tf_op jit(solution)/shard_map/dot_general | solution.py:169
  119.5 0.0 copy-done.3
  119.5 4.9 %fusion.11.v_ref = f32[4,96,256]{2,1,0:T(8,128)S(1)} fusion(bf16[4,96,4608]{2,1,0:T(8,128)(2,1)} %all-gather.4.cloned.1.call-done, f32[4608]{0:T(1024)S(1)} %copy-done.4, f32[4,96]{1,0:T(4,128)S(1)} %add_rsqrt_fusion, bf16[4608,256]{1,0:T(8,128)(2,1)} %param.21, bf16[4608,128]{0,1:T(8,128)(2,1)S(1)} %bitcast.42, bf16[1024,128]{0,1:T(8,128)(2,1)} %bitcast.50, ...), kind=kOutput, calls=%fused_computation.18 | convolution fusion | flops 1068761088 | bytes 6936584 | tf_op jit(solution)/shard_map/dot_general | solution.py:170
  124.4 0.0 copy-start.2
  124.4 7.0 %fusion.15.q_ref = f32[4,96,512]{2,1,0:T(8,128)S(1)} fusion(bf16[4,96,4608]{2,1,0:T(8,128)(2,1)} %all-gather.4.cloned.1.call-done, f32[4608]{0:T(1024)S(1)} %copy-done.4, f32[4,96]{1,0:T(4,128)S(1)} %add_rsqrt_fusion, bf16[4608,512]{1,0:T(8,128)(2,1)} %param.19, bf16[4608,128]{0,1:T(8,128)(2,1)} %bitcast.45, bf16[2048,128]{0,1:T(8,128)(2,1)} %bitcast.47, ...), kind=kOutput, calls=%fused_computation.20 | convolution fusion | flops 2130444288 | bytes 9719304 | tf_op jit(solution)/shard_map/dot_general | solution.py:168
  131.4 0.0 copy-done.2
  131.4 0.0 copy-start
  131.4 2.3 copy-done
  133.7 0.0 copy-start.1
  133.7 2.3 copy-done.1
  136.1 51.9 %shard_map.163 = bf16[4,96,512]{2,1,0:T(8,128)(2,1)S(1)} custom-call(s32[96]{0:T(128)S(1)} %copy-done.2, f32[4,96,512]{2,1,0:T(8,128)S(1)} %fusion.15.q_ref, f32[4,96,256]{2,1,0:T(8,128)S(1)} %fusion.13.k_ref, f32[4,96,256]{2,1,0:T(8,128)S(1)} %fusion.11.v_ref, f32[4,96,128]{2,1,0:T(8,128)S(1)} %get-tuple-element.10.cos_ref, ...), custom_call_target="tpu_custom_call" | custom-call | tf_op jit(solution)/shard_map/pallas_call | solution.py:117
  188.0 7.5 %convolution_convert_fusion = bf16[4,96,4608]{2,1,0:T(8,128)(2,1)} fusion(bf16[4,96,512]{2,1,0:T(8,128)(2,1)S(1)} %shard_map.163, bf16[512,4608]{1,0:T(8,128)(2,1)} %param.22, bf16[4608,128]{0,1:T(8,128)(2,1)S(1)} %bitcast.43, bf16[2048,128]{0,1:T(8,128)(2,1)} %bitcast.48, s32[]{:T(128)S(6)} %select_n.6), kind=kOutput, calls=%fused_computation.7 | convolution fusion | flops 2125135872 | bytes 9306116 | tf_op jit(solution)/shard_map/dot_general | solution.py:173
  195.5 8.0 %copy.18 = bf16[4,96,4608]{1,0,2:T(4,128)(2,1)} copy(bf16[4,96,4608]{2,1,0:T(8,128)(2,1)} %convolution_convert_fusion) | data formatting | bytes 7077888
  203.5 8.2 %reshape.54 = bf16[4608,384]{1,0:T(8,128)(2,1)} reshape(bf16[4608,4,96]{2,1,0:T(4,128)(2,1)} %bitcast.37) | data formatting | bytes 7077888
  211.7 0.0 reduce-scatter.4.cloned.1.call-update
  211.8 65.1 %reduce-scatter.4.cloned.1.call-done = bf16[1152,384]{1,0:T(8,128)(2,1)} async-done(((bf16[4608,384]{1,0:T(8,128)(2,1)}), bf16[1152,384]{1,0:T(8,128)(2,1)}) %reduce-scatter.4.cloned.1.call-update) | async-done | bytes 884752
  276.9 2.7 reshape.55
  279.6 1.9 copy.19
  (2 shorter events, 0.0 us)
Async XLA Ops:
  6.5 33.7 %all-gather.6.cloned.1.call-start = ((), (), s32[]{:S(2)}) async-start(), calls=%async_computation.2 | async-start | bytes 3932160 | tf_op jit(solution)/shard_map/all_gather | solution.py:148
  8.8 103.0 %all-gather.4.cloned.1.call-start = ((), (), s32[]{:S(2)}) async-start(), calls=%async_computation.1 | async-start | bytes 4423680 | tf_op jit(solution)/shard_map/all_gather | solution.py:149
  9.5 267.4 %reduce-scatter.4.cloned.1.call-start = ((), (), s32[]{:S(2)}) async-start(), calls=%async_computation.3 | async-start | bytes 4423680
  48.4 66.1 %copy-start.4 = (f32[4608]{0:T(1024)S(1)}, f32[4608]{0:T(1024)}, u32[]{:S(2)}) copy-start(f32[4608]{0:T(1024)} %convert_element_type.44) | copy-start | bytes 55300
  48.6 70.9 %copy-start.3 = (bf16[16,8,4,1152]{3,1,2,0:T(8,128)(2,1)}, bf16[16,8,4,1152]{3,1,2,0:T(8,128)(2,1)S(1)}, u32[]{:S(2)}) copy-start(bf16[16,8,4,1152]{3,1,2,0:T(8,128)(2,1)S(1)} %copy.20) | copy-start | bytes 3538948
  124.4 7.0 %copy-start.2 = (s32[96]{0:T(128)S(1)}, s32[96]{0:T(128)}, u32[]{:S(2)}) copy-start(s32[96]{0:T(128)} %lens_ref.1) | copy-start | bytes 1156
  131.4 2.3 copy-start
  133.7 2.3 copy-start.1
Sparse Core Ops, SparseCore 0:
  8.9 31.2 all-gather.5
  41.8 69.9 all-gather.3
  211.9 64.9 reduce-scatter.3
where the time goes:
time: 289 us; the launch traced here: 288 us
  waiting for transfers between devices  156 us (54%)
  Pallas kernels  51.9 us (18%)
  local copies, waits for them, and re-layouts  34.9 us (12%)
  matrix products  24.3 us (8%)
  between operations  13.3 us (5%)
  other arithmetic  7.91 us (3%)
    unnamed x4, waiting for transfers between devices  65.9 us
    all_gather x1, waiting for transfers between devices, shards(): xs = lax.all_gather(x, 'tp', axis=2, tiled=True)  62.2 us
    pallas_call x1, Pallas kernels, attention(): pl.pallas_call(functools.partial(attention_kernel, kv_local), out_shape=j...  51.9 us
    all_gather x1, waiting for transfers between devices, shards(): every = lax.all_gather(pack, 'fsdp', axis=0)  27.7 us
    unnamed x18, local copies, waits for them, and re-layouts  27.5 us
    dot_general x1, matrix products, shards(): terms = jnp.dot(attended, w_output, preferred_element_type=jnp.float32)  7.49 us
    dot_general x1, matrix products, shards(): q = jnp.dot(normed, w_query, preferred_element_type=jnp.float32)  6.97 us
    all_gather x1, local copies, waits for them, and re-layouts, shards(): every = lax.all_gather(pack, 'fsdp', axis=0)  6.26 us
  transfers between devices with their start and end apart: 3, of which 3 were waited for; matrix products, arithmetic and copies ran while one was open for 4% of the time, Pallas kernels for 0%

commit v1 on v0

v1 whole, which is shorter than its diff:
```python
import functools

import jax
import jax.numpy as jnp
from jax import lax
from jax.experimental import pallas as pl
from jax.experimental.pallas import tpu as pltpu
from jax.sharding import PartitionSpec as P

HEADS = 16
KV_HEADS = 8
HF = 128
STEPS = 4
CHUNK = 32

ADAPTER_SCALE = 2.0
SOFTCAP = 50.0
QUERY_SCALE = 144.0 ** (-0.5)
RMS_EPS = 1e-06
ROPE_BASE = 10000.0


def rope_tables(context_lengths):
    half = HF // 2
    freq = ROPE_BASE ** (-2.0 * jnp.arange(half, dtype=jnp.float32) / HF)
    steps = jnp.arange(STEPS, dtype=jnp.int32)
    position = (context_lengths[None, :] + steps[:, None]).astype(jnp.float32)
    angle = position[..., None] * freq
    cosine = jnp.cos(angle)
    sine = jnp.sin(angle)
    return (
        jnp.concatenate([cosine, cosine], axis=-1),
        jnp.concatenate([-sine, sine], axis=-1),
    )


MESH = pl.DeviceIdType.MESH
TOK = STEPS * CHUNK
NT = (((1,), (1,)), ((), ()))


def attend(kv_local, qkv, cos, sin, length, ckb, cvb, base, at, q3, k3, v3, a3):
    per = HEADS // KV_HEADS
    ql, kl = kv_local * per * HF, kv_local * HF
    for s in range(STEPS):
        c, n = cos(s), sin(s)
        rows = pl.ds(s * CHUNK, CHUNK)

        def rot(u):
            return u * c + pltpu.roll(u, HF // 2, 1) * n

        for g in range(kv_local):
            for p in range(per):
                u = qkv[rows, pl.ds((g * per + p) * HF, HF)]
                q3[:, g * 8 + s * per + p, :] = rot(u) * QUERY_SCALE
            k3[:, g * 8 + s, :] = rot(qkv[rows, pl.ds(ql + g * HF, HF)])
            v3[:, g * 8 + s, :] = qkv[rows, pl.ds(ql + kl + g * HF, HF)]

    slot = lax.broadcasted_iota(jnp.int32, (8, HF), 1)
    step_of = lax.broadcasted_iota(jnp.int32, (8, HF), 0) // per
    ctx = ckb.shape[2]
    new_live = (slot >= ctx) & (slot <= ctx + step_of)
    pad = jnp.zeros((HF - ctx - 8, HF), jnp.float32)
    group = 8

    def step(i, carry):
        pairs = [(i * group + j, g) for j in range(group) for g in range(kv_local)]

        def whole(cache, new, r, g):
            fresh = jnp.concatenate([new[r, pl.ds(g * 8, 8), :], pad]).astype(jnp.bfloat16)
            return jnp.concatenate([cache[base + r, g], fresh])

        scores = jnp.concatenate([
            lax.dot_general(
                q3[r, pl.ds(g * 8, 8), :].astype(jnp.bfloat16), whole(ckb, k3, r, g), NT,
                preferred_element_type=jnp.float32,
            )
            for r, g in pairs
        ])
        live = jnp.concatenate([
            jnp.where(new_live | (slot < length(base + r)), 1.0, 0.0) for r, g in pairs
        ])
        expo = jnp.exp(SOFTCAP * jnp.tanh(scores * (1.0 / SOFTCAP))) * live
        total = jnp.sum(expo, axis=-1, keepdims=True)
        weights = expo / total
        results = [
            jnp.dot(
                weights[8 * j:8 * j + 8].astype(jnp.bfloat16), whole(cvb, v3, r, g),
                preferred_element_type=jnp.float32,
            )
            for j, (r, g) in enumerate(pairs)
        ]
        for (r, g), result in zip(pairs, results):
            a3[r, pl.ds(g * 8, 8), :] = result
        return carry

    lax.fori_loop(0, CHUNK // group, step, 0)
    for s in range(STEPS):
        for g in range(kv_local):
            for p in range(per):
                at[pl.ds(s * CHUNK, CHUNK), pl.ds((g * per + p) * HF, HF)] = a3[
                    :, g * 8 + s * per + p, :
                ].astype(jnp.bfloat16)


def layer_kernel(
    n, n_fsdp, chunks, sizes, wo_split,
    lens, x, gain, wq, wk, wv, wo, pack, cos, sin, ck, cv, out,
    xall, fac, wqkv, wout, ckb, cvb, upqk, upv, odown, normed, qkv, at,
    q3, k3, v3, a3, parts, own, rlo, rhi, outb,
    ag_up, ag_dn, ag_rx, rs_up, rs_dn, rs_lo, rs_hi, fs_y, fs_p, fac_rx,
    x_sem, w_sem, kv_sem, pack_sem, out_sem,
):
    z = lax.axis_index("tp")
    f = lax.axis_index("fsdp")
    ny = n_fsdp // 2
    y, core = f // 2, f % 2
    partner = f + 1 - 2 * core
    m = n_fsdp // n
    s0, s2, s3 = sizes
    ql, kl = wq.shape[1], wk.shape[1]
    width = ql + 2 * kl
    kv_local = kl // HF
    dl = x.shape[2]

    def peer(dy):
        return ((y + dy) % ny) * 2 + core

    local = [
        pltpu.make_async_copy(x.at[:, pl.ds(c * CHUNK, CHUNK), :], xall.at[z, c], x_sem.at[c])
        for c in range(chunks)
    ]
    own_pack = pltpu.make_async_copy(pack, fac.at[f], pack_sem)
    weights = [
        pltpu.make_async_copy(wq, wqkv.at[:, pl.ds(0, ql)], w_sem.at[0]),
        pltpu.make_async_copy(wk, wqkv.at[:, pl.ds(ql, kl)], w_sem.at[1]),
        pltpu.make_async_copy(wv, wqkv.at[:, pl.ds(ql + kl, kl)], w_sem.at[2]),
    ]
    for p in range(n):
        piece = wo.at[p] if wo_split else wo.at[:, pl.ds(p * dl, dl)]
        weights.append(pltpu.make_async_copy(piece, wout.at[p], w_sem.at[3 + p]))
    caches = [
        pltpu.make_async_copy(ck, ckb, kv_sem.at[0]),
        pltpu.make_async_copy(cv, cvb, kv_sem.at[1]),
    ]
    for copy in local + [own_pack] + weights + caches:
        copy.start()

    barrier = pltpu.get_barrier_semaphore()

    def greet(target):
        pl.semaphore_signal(barrier, inc=1, device_id=target, device_id_type=MESH)

    @pl.when(z > 0)
    def _():
        greet({"tp": z - 1})

    @pl.when(z < n - 1)
    def _():
        greet({"tp": z + 1})

    for dy in range(1, ny):
        greet({"fsdp": peer(dy)})
    greet({"fsdp": partner})
    pl.semaphore_wait(barrier, ny + (z + n - 1) // n + (2 * n - 2 - z) // n)

    def ag(o, c, step):
        sem = ag_up if step > 0 else ag_dn
        return pltpu.make_async_remote_copy(
            src_ref=xall.at[o, c], dst_ref=xall.at[o, c], send_sem=sem.at[o, c],
            recv_sem=ag_rx.at[o, c], device_id={"tp": z + step}, device_id_type=MESH,
        )

    def ag_own(c):
        @pl.when(z < n - 1)
        def _():
            ag(z, c, 1).start()

        @pl.when(z > 0)
        def _():
            ag(z, c, -1).start()

    def ag_arrive(c, d):
        @pl.when(z - d >= 0)
        def _():
            ag(z - d, c, 1).wait_recv()

            @pl.when(z < n - 1)
            def _():
                ag(z - d, c, 1).start()

        @pl.when(z + d < n)
        def _():
            ag(z + d, c, -1).wait_recv()

            @pl.when(z > 0)
            def _():
                ag(z + d, c, -1).start()

    def fac_y(dy):
        return pltpu.make_async_remote_copy(
            src_ref=fac.at[f], dst_ref=fac.at[f], send_sem=fs_y.at[dy], recv_sem=fac_rx.at[f],
            device_id={"fsdp": peer(dy)}, device_id_type=MESH,
        )

    def fac_from(slot):
        return pltpu.make_async_remote_copy(
            src_ref=fac.at[slot], dst_ref=fac.at[slot], send_sem=fs_y.at[0],
            recv_sem=fac_rx.at[slot], device_id={"fsdp": partner}, device_id_type=MESH,
        )

    def fac_across(dy):
        slot = peer(dy)
        return pltpu.make_async_remote_copy(
            src_ref=fac.at[slot], dst_ref=fac.at[slot], send_sem=fs_p.at[dy],
            recv_sem=fac_rx.at[slot], device_id={"fsdp": partner}, device_id_type=MESH,
        )

    local[0].wait()
    ag_own(0)
    own_pack.wait()
    for dy in range(1, ny):
        fac_y(dy).start()
    fac_across(0).start()
    local[1].wait()
    ag_own(1)
    for c in range(2, chunks):
        local[c].wait()
    k3[...] = jnp.zeros_like(k3)
    v3[...] = jnp.zeros_like(v3)
    ag_arrive(0, 1)
    for dy in range(1, ny):
        fac_from(peer(dy)).wait_recv()
        fac_across(dy).start()
    for d in range(2, n - 1):
        ag_arrive(0, d)
    for c in range(2, chunks):
        ag_own(c)
    ag_arrive(1, 1)
    for dy in range(ny):
        fac_from(((y + dy) % ny) * 2 + 1 - core).wait_recv()

    def lanes(rows, high):
        lane = lax.broadcasted_iota(jnp.int32, (rows, HF), 1)
        return lane >= HF // 2 if high else lane < HF // 2

    def keep(value, high):
        wide = value.astype(jnp.float32)
        return jnp.where(lanes(value.shape[0], high), wide, 0.0).astype(jnp.bfloat16)

    for i in range(m):
        third = fac[z * m + i, pl.ds(2 * s0, s2), :]
        fourth = fac[z * m + i, pl.ds(2 * s0 + s2, s3), :]
        upqk[pl.ds(i * s2, s2), :] = keep(third, False)
        odown[pl.ds(i * s2, s2), :] = keep(third, True)
        upv[pl.ds(i * s3, s3), :] = keep(fourth, False)
        upqk[pl.ds(ql + i * s3, s3), :] = keep(fourth, True)

    for copy in weights[:3]:
        copy.wait()
    tile = 96
    tiles = s0 // tile

    def merge_in(i, carry):
        shard, t = i // tiles, i % tiles
        first = pl.ds(pl.multiple_of(t * tile, 32), tile)
        second = pl.ds(pl.multiple_of(s0 + t * tile, 32), tile)
        rows = pl.ds(pl.multiple_of(i * tile, 32), tile)
        a = lax.dot_general(fac[shard, first, :], upqk[...], NT, preferred_element_type=jnp.float32)
        b = lax.dot_general(fac[shard, second, :], upv[...], NT, preferred_element_type=jnp.float32)
        left, right = pl.ds(0, ql + kl), pl.ds(ql + kl, kl)
        wqkv[rows, left] = (wqkv[rows, left].astype(jnp.float32) + ADAPTER_SCALE * a).astype(jnp.bfloat16)
        wqkv[rows, right] = (wqkv[rows, right].astype(jnp.float32) + ADAPTER_SCALE * b).astype(jnp.bfloat16)
        return carry

    half = n_fsdp * tiles // 2
    lax.fori_loop(0, half, merge_in, 0)
    for d in range(2, n - 1):
        ag_arrive(1, d)
    lax.fori_loop(half, n_fsdp * tiles, merge_in, 0)
    if chunks > 2:
        ag_arrive(2, 1)
    for copy in weights[3:]:
        copy.wait()
    otile = 64
    otiles = ql // otile

    def merge_out(i, carry):
        p, t = i // otiles, i % otiles
        rows = pl.ds(pl.multiple_of(t * otile, otile), otile)
        up = jnp.concatenate([fac[p * m + j, pl.ds(s0, s0), :] for j in range(m)])
        a = lax.dot_general(odown[rows, :], up, NT, preferred_element_type=jnp.float32)
        wout[p, rows, :] = (wout[p, rows, :].astype(jnp.float32) + ADAPTER_SCALE * a).astype(jnp.bfloat16)
        return carry

    lax.fori_loop(0, n * otiles, merge_out, 0)
    for copy in caches:
        copy.wait()

    def rs(p, c, step):
        return pltpu.make_async_remote_copy(
            src_ref=parts.at[c, p], dst_ref=(rlo if step > 0 else rhi).at[c, p],
            send_sem=(rs_up if step > 0 else rs_dn).at[c, p],
            recv_sem=(rs_lo if step > 0 else rs_hi).at[c, p],
            device_id={"tp": z + step}, device_id_type=MESH,
        )

    def add_in(p, c, landed):
        parts[c, p] = (parts[c, p].astype(jnp.float32) + landed[c, p].astype(jnp.float32)).astype(jnp.bfloat16)

    def rs_first(c):
        @pl.when(z == 0)
        def _():
            for p in range(n - 1, 0, -1):
                rs(p, c, 1).start()

        @pl.when(z == n - 1)
        def _():
            for p in range(n - 1):
                rs(p, c, -1).start()

    def rs_forward(c):
        for k in range(1, n):
            up, dn = n - k, k - 1

            @pl.when((z > 0) & (z < up))
            def _():
                rs(up, c, 1).wait_recv()
                add_in(up, c, rlo)
                rs(up, c, 1).start()

            @pl.when((z < n - 1) & (z > dn))
            def _():
                rs(dn, c, -1).wait_recv()
                add_in(dn, c, rhi)
                rs(dn, c, -1).start()

    def out_copy(c):
        rows = pl.ds(pl.multiple_of(c * CHUNK, CHUNK), CHUNK)
        return pltpu.make_async_copy(outb.at[c], out.at[:, rows, :], out_sem.at[c])

    def rs_final(c):
        @pl.when(z > 0)
        def _():
            rs(z, c, 1).wait_recv()
            own[c] = own[c] + rlo[c, z].astype(jnp.float32)

        @pl.when(z < n - 1)
        def _():
            rs(z, c, -1).wait_recv()
            own[c] = own[c] + rhi[c, z].astype(jnp.float32)

        for s in range(STEPS):
            outb[c, s] = own[c, pl.ds(s * CHUNK, CHUNK), :].astype(jnp.bfloat16)
        out_copy(c).start()

    def chunk(c, carry):
        base = c * CHUNK
        ag_arrive(c, n - 1)
        for s in range(STEPS):
            square = jnp.zeros((CHUNK, 1), jnp.float32)
            for o in range(n):
                wide = xall[o, c, s].astype(jnp.float32)
                square += jnp.sum(wide * wide, axis=-1, keepdims=True)
            factor = lax.rsqrt(square * (1.0 / (n * dl)) + RMS_EPS)
            for o in range(n):
                wide = xall[o, c, s].astype(jnp.float32)
                normed[o, pl.ds(s * CHUNK, CHUNK), :] = (wide * factor * gain[o]).astype(jnp.bfloat16)

        def project(i, carry):
            cols = pl.ds(pl.multiple_of(i * 256, 256), 256)
            acc = jnp.zeros((TOK, 256), jnp.float32)
            for o in range(n):
                acc += jnp.dot(
                    normed[o], wqkv[pl.ds(o * dl, dl), cols], preferred_element_type=jnp.float32
                )
            qkv[:, cols] = acc
            return carry

        lax.fori_loop(0, width // 256, project, 0)

        if chunks > 2:
            @pl.when(c == 0)
            def _():
                for d in range(2, n - 1):
                    ag_arrive(2, d)

        @pl.when(c > 0)
        def _():
            rs_forward(c - 1)

        rows = pl.ds(pl.multiple_of(base, CHUNK), CHUNK)
        attend(
            kv_local, qkv, lambda s: cos[s, rows, :], lambda s: sin[s, rows, :],
            lambda r: lens[r], ckb, cvb, base, at, q3, k3, v3, a3,
        )

        @pl.when(c > 0)
        def _():
            rs_final(c - 1)

        def project_out(p, carry):
            terms = jnp.dot(at[...], wout[p], preferred_element_type=jnp.float32)
            parts[c, p] = terms.astype(jnp.bfloat16)

            @pl.when(p == z)
            def _():
                own[c] = terms

            return carry

        lax.fori_loop(0, n, project_out, 0)
        rs_first(c)
        return carry

    lax.fori_loop(0, chunks, chunk, 0)
    rs_forward(chunks - 1)
    rs_final(chunks - 1)

    for c in range(chunks):
        out_copy(c).wait()
        for o in range(n):
            @pl.when((o <= z) & (z < n - 1))
            def _():
                ag(o, c, 1).wait_send()

            @pl.when((o >= z) & (z > 0))
            def _():
                ag(o, c, -1).wait_send()

            @pl.when(o > z)
            def _():
                rs(o, c, 1).wait_send()

            @pl.when(o < z)
            def _():
                rs(o, c, -1).wait_send()

    for dy in range(1, ny):
        fac_y(dy).wait_send()
    for dy in range(ny):
        fac_across(dy).wait_send()


def shards(
    x, norm_gain, query_weight, key_weight, value_weight, output_weight,
    query_down, key_down, value_down, output_down,
    query_up, key_up_factor, value_up, output_up,
    cached_keys, cached_values, context_lengths,
):
    n, n_fsdp = lax.axis_size("tp"), lax.axis_size("fsdp")
    steps, nrows, dl = x.shape
    chunks = nrows // CHUNK
    ql, kl = query_weight.shape[1], key_weight.shape[1]
    d = n * dl
    kv_local = kl // HF
    sizes = (query_down.shape[0], output_down.shape[0], key_up_factor.shape[0])
    pack = jnp.concatenate([
        jnp.concatenate([query_down, key_down], 1),
        jnp.concatenate([value_down, output_up], 1),
        jnp.concatenate([query_up, output_down], 1),
        jnp.concatenate([value_up, key_up_factor], 1),
    ])
    gain = norm_gain.astype(jnp.float32).reshape(n, 1, dl)
    cos, sin = rope_tables(context_lengths)
    wo_split = dl % HF != 0
    if wo_split:
        output_weight = output_weight.reshape(ql, n, dl).transpose(1, 0, 2)
    bf, f32 = jnp.bfloat16, jnp.float32
    vm = pltpu.VMEM
    hbm = pl.BlockSpec(memory_space=pl.ANY)
    vmem = pl.BlockSpec(memory_space=pltpu.VMEM)
    smem = pl.BlockSpec(memory_space=pltpu.SMEM)
    heads = vm((CHUNK, kv_local * 8, HF), f32)
    block = vm((chunks, n, TOK, dl), bf)
    dma = pltpu.SemaphoreType.DMA
    return pl.pallas_call(
        functools.partial(layer_kernel, n, n_fsdp, chunks, sizes, wo_split),
        out_shape=jax.ShapeDtypeStruct((steps, nrows, dl), bf),
        in_specs=[smem, hbm, vmem, hbm, hbm, hbm, hbm, hbm, vmem, vmem, hbm, hbm],
        out_specs=hbm,
        scratch_shapes=[
            vm((n, chunks, STEPS, CHUNK, dl), bf),
            vm((n_fsdp,) + pack.shape, bf),
            vm((d, ql + 2 * kl), bf),
            vm((n, ql, dl), bf),
            vm(cached_keys.shape, bf),
            vm(cached_values.shape, bf),
            vm((ql + kl, HF), bf),
            vm((kl, HF), bf),
            vm((ql, HF), bf),
            vm((n, TOK, dl), bf),
            vm((TOK, ql + 2 * kl), f32),
            vm((TOK, ql), bf),
            heads, heads, heads, heads,
            block,
            vm((chunks, TOK, dl), f32),
            block, block,
            vm((chunks, STEPS, CHUNK, dl), bf),
            dma((n, chunks)), dma((n, chunks)), dma((n, chunks)),
            dma((chunks, n)), dma((chunks, n)), dma((chunks, n)), dma((chunks, n)),
            dma((n_fsdp // 2,)), dma((n_fsdp // 2,)), dma((n_fsdp,)),
            dma((chunks,)), dma((3 + n,)), dma((2,)), dma(()), dma((chunks,)),
        ],
        compiler_params=pltpu.CompilerParams(
            collective_id=0, has_side_effects=True, vmem_limit_bytes=60 * 2**20
        ),
    )(
        context_lengths, x, gain, query_weight, key_weight, value_weight, output_weight,
        pack, cos, sin, cached_keys, cached_values,
    )


def solution(mesh):
    fs = ("groups", "fsdp")
    return jax.shard_map(
        shards,
        mesh=mesh,
        in_specs=(
            P(None, fs, "tp"), P(),
            P(None, "tp"), P(None, "tp"), P(None, "tp"), P("tp", None),
            P(fs, None), P(fs, None), P(fs, None), P(fs, None),
            P(fs, None), P(fs, None), P(fs, None), P(fs, None),
            P(fs, "tp", None, None), P(fs, "tp", None, None), P(fs),
        ),
        out_specs=P(None, fs, "tp"),
        check_vma=False,
    )
```

time: 289 us -> 164 us (0.57)
  waiting for transfers between devices: 156 us -> 0 us
  Pallas kernels: 51.9 us -> 151 us
  local copies, waits for them, and re-layouts: 34.9 us -> 9.9 us
  matrix products: 24.3 us -> 0 us
  between operations: 13.3 us -> 0.06 us
  other arithmetic: 7.91 us -> 3.03 us
    pallas_call x1, Pallas kernels: 51.9 us -> 151 us  [shards(): pl.pallas_call(functools.partial(layer_kernel, n, n_fsdp, chunks, sizes,...]
    all_gather x2 -> x0, waiting for transfers between devices: 89.9 us -> none  [the longest x1 62.2 us: shards(): xs = lax.all_gather(x, 'tp', axis=2, tiled=True)]
    unnamed x4 -> x0, waiting for transfers between devices: 65.9 us -> none
    dot_general x4 -> x0, matrix products: 24.3 us -> none  [the longest x1 7.49 us: shards(): terms = jnp.dot(attended, w_output, preferred_element_type=jnp.float32)]
    unnamed x18 -> x15, local copies, waits for them, and re-layouts: 27.5 us -> 8.53 us
    all_gather x1 -> x0, local copies, waits for them, and re-layouts: 6.26 us -> none  [shards(): every = lax.all_gather(pack, 'fsdp', axis=0)]
  transfers between devices with their start and end apart: 3 -> 0, of which waited for: 3 -> 0; matrix products, arithmetic and copies ran while one was open for 4% -> 0% of each run, Pallas kernels for 0% -> 0%
where the time goes in v1:
time: 164 us
  Pallas kernels  151 us (92%)
  local copies, waits for them, and re-layouts  9.9 us (6%)
  other arithmetic  3.03 us (2%)
    pallas_call x1, Pallas kernels, shards(): pl.pallas_call(functools.partial(layer_kernel, n, n_fsdp, chunks, sizes,...  151 us
    unnamed x15, local copies, waits for them, and re-layouts  8.53 us

profile of v1, /device:TPU:0, one launch (start us, length us, event | category | flops | bytes accessed | tf_op | source)
XLA Modules:
  0.0 163.6 jit_solution(11021072650180058183)
XLA Ops:
  0.0 0.0 copy-start
  0.0 0.0 copy-start.1
  0.0 1.4 reshape.32.gain
  1.4 0.9 copy.25
  2.2 0.9 copy.24
  3.1 1.0 copy.23
  4.1 1.0 copy.22
  5.1 1.1 copy.21
  6.2 1.1 copy.20
  7.3 0.0 copy-done
  7.3 0.0 copy-start.2
  7.3 0.2 copy.19
  7.6 0.0 copy-done.1
  7.6 0.2 copy.18
  7.8 1.3 maximum_maximum_fusion.pack
  9.1 0.0 copy-done.2
  9.1 0.8 fusion
  9.9 0.9 pad_maximum_fusion
  10.8 150.6 %shard_map.163 = bf16[4,96,1152]{2,1,0:T(8,128)(2,1)} custom-call(s32[96]{0:T(128)} %lens.1, bf16[4,96,1152]{2,1,0:T(8,128)(2,1)} %x.1, f32[4,1,1152]{2,1,0:T(1,128)} %reshape.32.gain, bf16[4608,512]{1,0:T(8,128)(2,1)} %wq.1, bf16[4608,256]{1,0:T(8,128)(2,1)} %wk.1, bf16[4608,256]{1,0:T(8,128)(2,1)} %wv.1, bf16[512,4608]{1,0:T(8,128)(2,1)} %wo.1, ...), custom_call_target="tpu_custom_call" | custom-call | tf_op jit(solution)/shard_map/pallas_call | solution.py:477
  161.4 2.1 %copy.27 = bf16[4,96,1152]{2,1,0:T(8,128)(2,1)} copy(bf16[4,96,1152]{2,1,0:T(8,128)(2,1)} %shard_map.163) | data formatting | bytes 1769472
  (2 shorter events, 0.0 us)
Async XLA Ops:
  0.0 7.3 %copy-start = (bf16[1152,64]{0,1:T(8,128)(2,1)S(1)}, bf16[1152,64]{0,1:T(8,128)(2,1)}, u32[]{:S(2)}) copy-start(bf16[1152,64]{0,1:T(8,128)(2,1)} %param.24) | copy-start | bytes 442372
  0.0 7.6 %copy-start.1 = (bf16[1152,64]{0,1:T(8,128)(2,1)S(1)}, bf16[1152,64]{0,1:T(8,128)(2,1)}, u32[]{:S(2)}) copy-start(bf16[1152,64]{0,1:T(8,128)(2,1)} %param.23) | copy-start | bytes 442372
  7.3 1.8 %copy-start.2 = (s32[96]{0:T(128)S(1)}, s32[96]{0:T(128)}, u32[]{:S(2)}) copy-start(s32[96]{0:T(128)} %lens.1) | copy-start | bytes 1156
